TPU v7x, 256 devices: a whole 4x4x8 slice. The times are simulated.
256 devices in a mesh: dp: 32 (over z, x), mp: 8 (over y, core).
Axes of the slice: x: 4, y: 4, z: 8, core: 2. Of those that a mesh axis runs over, the one named last changes fastest.
Arguments:
- tokens: bfloat16 [12288, 8192], P('dp', 'mp'), may hold values from -6 to 6
- frozen_base_weight: bfloat16 [8192, 8192], P('mp', 'dp'), may hold values from -0.0625 to 0.0625
- tenant_down_factors: bfloat16 [64, 8192, 64], P('dp', 'mp'), may hold values from -0.0625 to 0.0625
- tenant_up_factors: bfloat16 [64, 8192, 64], P('dp', 'mp'), may hold values from -0.75 to 0.75
- cotangent: bfloat16 [12288, 8192], P('dp', 'mp'), may hold values from -6 to 6
- block_tenant_index: int32 [96], replicated, may hold values from 0 to 63
- ranks: int32 [64], replicated, may hold values from 8 to 64
Outputs:
- layer_out: bfloat16 [12288, 8192], P('dp', 'mp')
- input_grad: bfloat16 [12288, 8192], P('dp', 'mp')
- down_grad: float32 [64, 8192, 64], P('dp', 'mp')
- up_grad: float32 [64, 8192, 64], P('dp', 'mp')
Inputs may be any that keep to these rules, and one draw needn't show every extreme that they name: `block_tenant_index`: tenant of each block of 128 consecutive rows; some tenants own many blocks, some none. `ranks`: rank columns at or past a tenant's rank are unused.
All inputs are finite; a program needn't handle non-finite values.
Results may differ from a plain program's by a relative error of at most 0.017.
Values may be sent and summed in bfloat16 or wider, within the bound.
A program may use at most 128 MiB of HBM per device.

v0:
```python
import jax
import jax.numpy as jnp
from jax import lax
from jax.sharding import PartitionSpec as P

BLOCK = 128


def local(
    tokens,
    frozen_base_weight,
    tenant_down_factors,
    tenant_up_factors,
    cotangent,
    block_tenant_index,
    ranks,
):
    num_peers = lax.axis_size("dp")
    my_index = lax.axis_index("dp")
    row_count, feat_width = tokens.shape
    block_count = row_count // BLOCK
    held_tenant_count = tenant_down_factors.shape[0]
    rank_padding = tenant_down_factors.shape[2]
    count_of_tenants = held_tenant_count * num_peers
    piece_width = feat_width // num_peers
    block_total = block_count * num_peers
    rank_positions = jnp.arange(rank_padding, dtype=jnp.int32)
    kept_ranks = (rank_positions[None, :] < ranks[:, None]).astype(jnp.float32)
    coef_table = kept_ranks * (16.0 / ranks.astype(jnp.float32))[:, None]
    tenant_range = jnp.arange(count_of_tenants, dtype=jnp.int32)
    my_tenants = lax.dynamic_slice_in_dim(block_tenant_index, my_index * block_count, block_count)
    select_onehot = (my_tenants[:, None] == tenant_range[None, :]).astype(jnp.float32)
    block_coef = jnp.dot(select_onehot, coef_table, precision=lax.Precision.HIGHEST)
    stacked_factors = jnp.concatenate([tenant_down_factors, tenant_up_factors], axis=2)
    split_factors = stacked_factors.reshape(
        held_tenant_count, num_peers, piece_width, 2 * rank_padding
    )
    received = lax.all_to_all(split_factors, "dp", split_axis=1, concat_axis=0, tiled=True)
    piece_table = received.reshape(count_of_tenants, piece_width * 2 * rank_padding)
    selection = block_tenant_index.reshape(num_peers, block_count)
    outgoing = piece_table[selection].reshape(num_peers, block_count, piece_width, 2 * rank_padding)
    arrived = lax.all_to_all(outgoing, "dp", split_axis=0, concat_axis=2, tiled=True)
    factors = arrived.reshape(block_count, feat_width, 2 * rank_padding)
    down_factor = factors[:, :, :rank_padding]
    up_factor = factors[:, :, rank_padding:]
    tok_blocks = tokens.reshape(block_count, BLOCK, feat_width)
    low_partial = jnp.einsum(
        "bid,bdr->bir", tok_blocks, down_factor, preferred_element_type=jnp.float32
    )
    pre_low = lax.psum(low_partial.astype(jnp.bfloat16), "mp").astype(jnp.float32)
    low_rank = (pre_low * block_coef[:, None, :]).astype(jnp.bfloat16)
    weights_all = lax.all_gather(frozen_base_weight, "dp", axis=1, tiled=True)
    base_terms = jnp.dot(tokens, weights_all, preferred_element_type=jnp.float32)
    base_share = lax.psum_scatter(
        base_terms.astype(jnp.bfloat16), "mp", scatter_dimension=1, tiled=True
    ).astype(jnp.float32)
    adapter_out = jnp.einsum(
        "bir,ber->bie", low_rank, up_factor, preferred_element_type=jnp.float32
    )
    layer_out = (base_share + adapter_out.reshape(row_count, feat_width)).astype(jnp.bfloat16)
    cot_blocks = cotangent.reshape(block_count, BLOCK, feat_width)
    dlow_partial = jnp.einsum(
        "bie,ber->bir", cot_blocks, up_factor, preferred_element_type=jnp.float32
    )
    pre_dlow = lax.psum(dlow_partial.astype(jnp.bfloat16), "mp").astype(jnp.float32)
    dlow_rank = (pre_dlow * block_coef[:, None, :]).astype(jnp.bfloat16)
    full_cotangent = lax.all_gather(cotangent, "mp", axis=1, tiled=True)
    base_grad = lax.dot_general(
        full_cotangent, weights_all, (((1,), (1,)), ((), ())), preferred_element_type=jnp.float32
    )
    adapter_grad = jnp.einsum(
        "bir,bdr->bid", dlow_rank, down_factor, preferred_element_type=jnp.float32
    )
    input_grad = (base_grad + adapter_grad.reshape(row_count, feat_width)).astype(jnp.bfloat16)
    block_down = jnp.einsum(
        "bid,bir->bdr", tok_blocks, dlow_rank, preferred_element_type=jnp.float32
    )
    block_up = jnp.einsum("bie,bir->ber", cot_blocks, low_rank, preferred_element_type=jnp.float32)
    block_grads = jnp.concatenate([block_down, block_up], axis=2)
    split_grads = block_grads.reshape(block_count, num_peers, piece_width, 2 * rank_padding)
    grad_arrived = lax.all_to_all(
        split_grads.astype(jnp.bfloat16), "dp", split_axis=1, concat_axis=0, tiled=True
    ).astype(split_grads.dtype)
    grad_rows = grad_arrived.reshape(block_total, piece_width * 2 * rank_padding)
    tenant_onehot = (block_tenant_index[None, :] == tenant_range[:, None]).astype(jnp.float32)
    tenant_sums = jnp.dot(tenant_onehot, grad_rows, precision=lax.Precision.HIGHEST)
    owner_bound = tenant_sums.reshape(num_peers, held_tenant_count, piece_width, 2 * rank_padding)
    owned_grads = lax.all_to_all(
        owner_bound.astype(jnp.bfloat16), "dp", split_axis=0, concat_axis=2, tiled=True
    ).astype(owner_bound.dtype)
    owned_grads = owned_grads.reshape(held_tenant_count, feat_width, 2 * rank_padding)
    down_grad = owned_grads[:, :, :rank_padding]
    up_grad = owned_grads[:, :, rank_padding:]
    return (layer_out, input_grad, down_grad, up_grad)


def solution(mesh):
    return jax.shard_map(
        local,
        mesh=mesh,
        in_specs=(
            P("dp", "mp"),
            P("mp", "dp"),
            P("dp", "mp", None),
            P("dp", "mp", None),
            P("dp", "mp"),
            P(),
            P(),
        ),
        out_specs=(P("dp", "mp"), P("dp", "mp"), P("dp", "mp", None), P("dp", "mp", None)),
        check_vma=False,
    )
```

profile of v0, /device:TPU:8, one launch (start us, length us, event | category | flops | bytes accessed | tf_op | source)
XLA Modules:
  0.0 286.6 jit_solution(3312873384921859337)
XLA Ops:
  8.0 0.0 copy-start
  8.0 0.0 all-gather.3.cloned.1.call-start
  8.1 0.7 all-gather.3.cloned.1.call-update
  8.7 1.2 copy.26
  10.0 1.2 copy.25
  11.2 0.3 pad_maximum_fusion.1
  11.5 0.9 copy.27
  12.4 11.3 %all-to-all-start = ((bf16[2,32,32,128]{3,2,0,1:T(8,128)(2,1)}), bf16[2,32,32,128]{3,2,0,1:T(8,128)(2,1)S(1)}, u32[]{:S(2)}, u32[]{:S(2)}) async-start(bf16[2,32,32,128]{3,2,0,1:T(8,128)(2,1)} %copy.27), calls=%async_computation.1 | async-start | bytes 1048576 | tf_op jit(solution)/shard_map/all_to_all | solution.py:38
  23.7 0.0 all-reduce.3.cloned.1.call-start
  23.7 0.8 reshape.107
  24.5 0.1 reshape.119
  24.6 20.3 %all-to-all-done = bf16[2,32,32,128]{3,2,0,1:T(8,128)(2,1)S(1)} async-done(((bf16[2,32,32,128]{3,2,0,1:T(8,128)(2,1)}), bf16[2,32,32,128]{3,2,0,1:T(8,128)(2,1)S(1)}, u32[]{:S(2)}, u32[]{:S(2)}) %all-to-all-start) | async-done | bytes 524320 | tf_op jit(solution)/shard_map/all_to_all | solution.py:38
  44.9 0.2 copy.54
  45.1 0.0 copy-start.1
  45.1 1.0 gather_fusion
  46.2 0.2 copy.43
  46.3 30.9 %all_to_all.54 = bf16[32,3,32,128]{3,2,1,0:T(8,128)(2,1)S(1)} all-to-all(bf16[32,3,32,128]{3,2,1,0:T(8,128)(2,1)S(1)} %bitcast.90), channel_id=1, replica_groups=mesh['dp'=32,'mp'=8] {'dp'}, dimensions={0} | all-to-all | bytes 1572864 | tf_op jit(solution)/shard_map/all_to_all | solution.py:42
  77.2 0.1 copy.28
  77.3 0.0 copy-done
  77.3 1.1 fusion.4
  78.3 0.0 copy-done.1
  78.3 1.4 fusion.5
  79.8 0.0 all-reduce.3.cloned.1.call-update
  79.8 0.0 all-gather.5.cloned.1.call-start
  79.9 0.7 all-gather.5.cloned.1.call-update
  80.6 0.0 reduce-scatter.2.cloned.1.call-start
  80.6 103.5 %all-gather.3.cloned.1.call-done = bf16[1024,8192]{1,0:T(8,128)(2,1)} async-done(((bf16[1024,256]{1,0:T(8,128)(2,1)}), bf16[1024,8192]{1,0:T(8,128)(2,1)}) %all-gather.3.cloned.1.call-update) | async-done | bytes 16777232 | tf_op jit(solution)/shard_map/all_gather | solution.py:52
  184.1 14.3 %convolution_convert_fusion = bf16[384,8192]{1,0:T(8,128)(2,1)} fusion(bf16[384,1024]{1,0:T(8,128)(2,1)S(1)} %copy-done, bf16[1024,8192]{1,0:T(8,128)(2,1)} %all-gather.3.cloned.1.call-done), kind=kOutput, calls=%fused_computation.1 | convolution fusion | flops 6445596672 | bytes 23855104 | tf_op jit(solution)/shard_map/dot_general | solution.py:53
  198.4 0.0 copy-start.5
  198.4 0.0 copy-start.6
  198.4 0.0 copy-start.2
  198.4 0.0 reduce-scatter.2.cloned.1.call-update
  198.5 0.6 copy-done.5
  199.1 0.1 dynamic_slice.3
  199.2 0.0 copy-done.6
  199.2 0.2 fusion.13
  199.4 0.0 all-reduce.3.cloned.1.call-done
  199.4 0.0 copy-start.4
  199.4 0.2 copy-done.2
  199.6 1.1 fusion.3
  200.7 1.1 fusion.2
  201.8 0.0 copy-start.3
  201.8 0.1 pad_maximum_fusion
  201.9 0.4 copy.31
  202.3 0.9 copy.32
  203.2 5.5 %all-to-all-start.2 = ((bf16[3,32,32,128]{3,2,0,1:T(8,128)(2,1)}), bf16[3,32,32,128]{3,2,0,1:T(8,128)(2,1)S(1)}, u32[]{:S(2)}, u32[]{:S(2)}) async-start(bf16[3,32,32,128]{3,2,0,1:T(8,128)(2,1)} %copy.32), calls=%async_computation.3 | async-start | bytes 1572864 | tf_op jit(solution)/shard_map/all_to_all | solution.py:81
  208.8 20.0 %all-to-all-done.2 = bf16[3,32,32,128]{3,2,0,1:T(8,128)(2,1)S(1)} async-done(((bf16[3,32,32,128]{3,2,0,1:T(8,128)(2,1)}), bf16[3,32,32,128]{3,2,0,1:T(8,128)(2,1)S(1)}, u32[]{:S(2)}, u32[]{:S(2)}) %all-to-all-start.2) | async-done | bytes 786464 | tf_op jit(solution)/shard_map/all_to_all | solution.py:81
  228.8 0.4 convolution_convert_fusion.1
  229.2 1.0 copy.34
  230.2 5.3 %all-to-all-start.3 = ((bf16[32,2,32,128]{3,2,1,0:T(8,128)(2,1)}), bf16[32,2,32,128]{3,2,1,0:T(8,128)(2,1)}, u32[]{:S(2)}, u32[]{:S(2)}) async-start(bf16[32,2,32,128]{3,2,1,0:T(8,128)(2,1)} %copy.34), calls=%async_computation.4 | async-start | bytes 1048576 | tf_op jit(solution)/shard_map/all_to_all | solution.py:88
  235.4 0.0 copy-done.4
  235.5 0.7 fusion.7
  236.2 0.0 copy-done.3
  236.2 1.7 fusion.11
  237.9 12.4 %all-to-all-done.3 = bf16[32,2,32,128]{3,2,1,0:T(8,128)(2,1)} async-done(((bf16[32,2,32,128]{3,2,1,0:T(8,128)(2,1)}), bf16[32,2,32,128]{3,2,1,0:T(8,128)(2,1)}, u32[]{:S(2)}, u32[]{:S(2)}) %all-to-all-start.3) | async-done | bytes 524320 | tf_op jit(solution)/shard_map/all_to_all | solution.py:88
  250.3 1.2 bitcast_convert_fusion
  251.5 1.6 fusion.24
  253.1 2.3 copy.36
  255.5 2.3 copy.37
  257.8 0.0 all-gather.5.cloned.1.call-done
  257.8 19.0 %fusion = bf16[384,1024]{1,0:T(8,128)(2,1)} fusion(f32[3,128,1024]{2,1,0:T(8,128)} %fusion.11, bf16[384,8192]{1,0:T(8,128)(2,1)} %all-gather.5.cloned.1.call-done, bf16[1024,8192]{1,0:T(8,128)(2,1)} %all-gather.3.cloned.1.call-done), kind=kOutput, calls=%fused_computation.3 | convolution fusion | flops 6443237376 | bytes 25427968 | tf_op jit(solution)/shard_map/dot_general | solution.py:68
  276.8 0.0 reduce-scatter.2.cloned.1.call-done
  276.8 2.4 fusion.1
  (4 shorter events, 0.0 us)
Async XLA Ops:
  8.0 69.3 %copy-start = (bf16[384,1024]{1,0:T(8,128)(2,1)S(1)}, bf16[384,1024]{1,0:T(8,128)(2,1)}, u32[]{:S(2)}) copy-start(bf16[384,1024]{1,0:T(8,128)(2,1)} %param.7) | copy-start | bytes 2359300
  8.0 176.1 %all-gather.3.cloned.1.call-start = ((), (), s32[]{:S(2)}) async-start(), calls=%async_computation.5 | async-start | bytes 17301504 | tf_op jit(solution)/shard_map/all_gather | solution.py:52
  12.4 32.5 %all-to-all-start = ((bf16[2,32,32,128]{3,2,0,1:T(8,128)(2,1)}), bf16[2,32,32,128]{3,2,0,1:T(8,128)(2,1)S(1)}, u32[]{:S(2)}, u32[]{:S(2)}) async-start(bf16[2,32,32,128]{3,2,0,1:T(8,128)(2,1)} %copy.27), calls=%async_computation.1 | async-start | bytes 1048576 | tf_op jit(solution)/shard_map/all_to_all | solution.py:38
  23.7 175.7 %all-reduce.3.cloned.1.call-start = ((), (), s32[]{:S(2)}) async-start(), calls=%async_computation.8 | async-start | bytes 196608 | tf_op jit(solution)/shard_map/psum | solution.py:50
  45.1 33.2 %copy-start.1 = (bf16[384,1024]{1,0:T(8,128)(2,1)S(1)}, bf16[384,1024]{1,0:T(8,128)(2,1)}, u32[]{:S(2)}) copy-start(bf16[384,1024]{1,0:T(8,128)(2,1)} %param.11) | copy-start | bytes 2359300
  79.8 178.0 %all-gather.5.cloned.1.call-start = ((), (), s32[]{:S(2)}) async-start(), calls=%async_computation.7 | async-start | bytes 7077888 | tf_op jit(solution)/shard_map/all_gather | solution.py:67
  80.6 196.3 %reduce-scatter.2.cloned.1.call-start = ((), (), s32[]{:S(2)}) async-start(), calls=%async_computation.6 | async-start | bytes 7077888 | tf_op jit(solution)/shard_map/reduce_scatter | solution.py:54
  198.4 0.7 copy-start.5
  198.4 0.7 copy-start.6
  198.4 1.2 copy-start.2
  199.4 36.1 %copy-start.4 = (bf16[3,128,64]{1,2,0:T(8,128)(2,1)S(1)}, bf16[3,128,64]{1,2,0:T(8,128)(2,1)}, u32[]{:S(2)}) copy-start(bf16[3,128,64]{1,2,0:T(8,128)(2,1)} %get-tuple-element.12) | copy-start | bytes 147460
  201.8 34.4 %copy-start.3 = (bf16[3,128,64]{1,2,0:T(8,128)(2,1)S(1)}, bf16[3,128,64]{1,2,0:T(8,128)(2,1)}, u32[]{:S(2)}) copy-start(bf16[3,128,64]{1,2,0:T(8,128)(2,1)} %get-tuple-element.13) | copy-start | bytes 147460
  203.2 25.6 %all-to-all-start.2 = ((bf16[3,32,32,128]{3,2,0,1:T(8,128)(2,1)}), bf16[3,32,32,128]{3,2,0,1:T(8,128)(2,1)S(1)}, u32[]{:S(2)}, u32[]{:S(2)}) async-start(bf16[3,32,32,128]{3,2,0,1:T(8,128)(2,1)} %copy.32), calls=%async_computation.3 | async-start | bytes 1572864 | tf_op jit(solution)/shard_map/all_to_all | solution.py:81
  230.2 20.2 %all-to-all-start.3 = ((bf16[32,2,32,128]{3,2,1,0:T(8,128)(2,1)}), bf16[32,2,32,128]{3,2,1,0:T(8,128)(2,1)}, u32[]{:S(2)}, u32[]{:S(2)}) async-start(bf16[32,2,32,128]{3,2,1,0:T(8,128)(2,1)} %copy.34), calls=%async_computation.4 | async-start | bytes 1048576 | tf_op jit(solution)/shard_map/all_to_all | solution.py:88
Sparse Core Ops, SparseCore 0:
  11.6 172.4 all-gather.2
  186.1 47.7 all-gather.4
Sparse Core Ops, SparseCore 1:
  79.9 59.3 all-reduce.2
  198.5 54.7 reduce-scatter.1
where the time goes:
time: 287 us
  waiting for transfers between devices  158 us (55%)
  matrix products  41.1 us (14%)
  blocking collectives  30.9 us (11%)
  starting transfers between devices  22.3 us (8%)
  between operations  15.7 us (5%)
  local copies, waits for them, and re-layouts  15.2 us (5%)
  other arithmetic  3.91 us (1%)
    all_gather x1, waiting for transfers between devices, local(): weights_all = lax.all_gather(frozen_base_weight, 'dp', axis=1, tiled=True)  103 us
    all_to_all x1, blocking collectives, local(): lax.all_to_all(outgoing, 'dp', split_axis=0, concat_axis=2, tiled=True)  30.9 us
    all_to_all x1, waiting for transfers between devices, local(): lax.all_to_all(split_factors, 'dp', split_axis=1, concat_axis=0, tiled=True)  20.3 us
    all_to_all x1, waiting for transfers between devices, local(): lax.all_to_all(split_grads.astype(jnp.bfloat16), 'dp', split_axis=1, conc...  20 us
    dot_general x1, matrix products, local(): lax.dot_general(full_cotangent, weights_all, (((1,), (1,)), ((), ())), pr...  19 us
    dot_general x1, matrix products, local(): jnp.dot(tokens, weights_all, preferred_element_type=jnp.float32)  14.3 us
    all_to_all x1, waiting for transfers between devices, local(): lax.all_to_all(owner_bound.astype(jnp.bfloat16), 'dp', split_axis=0, conc...  12.4 us
    all_to_all x1, starting transfers between devices, local(): lax.all_to_all(split_factors, 'dp', split_axis=1, concat_axis=0, tiled=True)  11.3 us
  transfers between devices with their start and end apart: 7, of which 4 were waited for; matrix products, arithmetic and copies ran while one was open for 20% of the time, Pallas kernels for 0%

commit v1 on v0

--- a/solution.py
+++ b/solution.py
@@ -4,6 +4,13 @@
 from jax.sharding import PartitionSpec as P
 
 BLOCK = 128
+
+
+def exchange_blocks(block, axis, split, join):
+    devices = lax.axis_size(axis)
+    parts = jnp.stack(jnp.split(block, devices, axis=split), axis=0)
+    parts = lax.all_to_all(parts, axis, split_axis=0, concat_axis=0)
+    return jnp.concatenate(parts, axis=join)
 
 
 def local(
@@ -85,9 +92,9 @@
     tenant_onehot = (block_tenant_index[None, :] == tenant_range[:, None]).astype(jnp.float32)
     tenant_sums = jnp.dot(tenant_onehot, grad_rows, precision=lax.Precision.HIGHEST)
     owner_bound = tenant_sums.reshape(num_peers, held_tenant_count, piece_width, 2 * rank_padding)
-    owned_grads = lax.all_to_all(
-        owner_bound.astype(jnp.bfloat16), "dp", split_axis=0, concat_axis=2, tiled=True
-    ).astype(owner_bound.dtype)
+    owned_grads = exchange_blocks(owner_bound.astype(jnp.bfloat16), "dp", 0, 2).astype(
+        owner_bound.dtype
+    )
     owned_grads = owned_grads.reshape(held_tenant_count, feat_width, 2 * rank_padding)
     down_grad = owned_grads[:, :, :rank_padding]
     up_grad = owned_grads[:, :, rank_padding:]

time: 287 us -> 336 us (1.17)
  waiting for transfers between devices: 158 us -> 181 us
  local copies, waits for them, and re-layouts: 15.2 us -> 36.5 us
  starting transfers between devices: 22.3 us -> 28.3 us
  blocking collectives: 30.9 us -> 26.3 us
    psum x1, waiting for transfers between devices: 0.01 us -> 56.7 us  [local(): lax.psum(low_partial.astype(jnp.bfloat16), 'mp').astype(jnp.float32)]
    all_gather x1, waiting for transfers between devices: 103 us -> 63.4 us  [local(): weights_all = lax.all_gather(frozen_base_weight, 'dp', axis=1, tiled=True)]
    unnamed x20 -> x51, local copies, waits for them, and re-layouts: 8.36 us -> 27.7 us
    all_to_all x1, waiting for transfers between devices: 20 us -> 30.5 us  [local(): lax.all_to_all(split_grads.astype(jnp.bfloat16), 'dp', split_axis=1, conc...]
    all_to_all x1, blocking collectives: 30.9 us -> 26.3 us  [local(): lax.all_to_all(outgoing, 'dp', split_axis=0, concat_axis=2, tiled=True)]
    all_to_all x1, starting transfers between devices: 5.54 us -> 9.54 us  [local(): lax.all_to_all(split_grads.astype(jnp.bfloat16), 'dp', split_axis=1, conc...]
    all_to_all x1, waiting for transfers between devices: 20.3 us -> 16.8 us  [local(): lax.all_to_all(split_factors, 'dp', split_axis=1, concat_axis=0, tiled=True)]
  transfers between devices with their start and end apart: 7 -> 7, of which waited for: 4 -> 5; matrix products, arithmetic and copies ran while one was open for 20% -> 21% of each run, Pallas kernels for 0% -> 0%
where the time goes in v1:
time: 336 us; the launch traced here: 334 us
  waiting for transfers between devices  181 us (54%)
  matrix products  41.4 us (12%)
  local copies, waits for them, and re-layouts  36.5 us (11%)
  starting transfers between devices  28.3 us (8%)
  blocking collectives  26.3 us (8%)
  between operations  15.8 us (5%)
  other arithmetic  3.91 us (1%)
    all_gather x1, waiting for transfers between devices, local(): weights_all = lax.all_gather(frozen_base_weight, 'dp', axis=1, tiled=True)  63.4 us
    psum x1, waiting for transfers between devices, local(): lax.psum(low_partial.astype(jnp.bfloat16), 'mp').astype(jnp.float32)  56.7 us
    all_to_all x1, waiting for transfers between devices, local(): lax.all_to_all(split_grads.astype(jnp.bfloat16), 'dp', split_axis=1, conc...  30.5 us
    unnamed x51, local copies, waits for them, and re-layouts  27.7 us
    all_to_all x1, blocking collectives, local(): lax.all_to_all(outgoing, 'dp', split_axis=0, concat_axis=2, tiled=True)  26.3 us
    dot_general x1, matrix products, local(): lax.dot_general(full_cotangent, weights_all, (((1,), (1,)), ((), ())), pr...  19.4 us
    all_to_all x1, waiting for transfers between devices, local(): lax.all_to_all(split_factors, 'dp', split_axis=1, concat_axis=0, tiled=True)  16.8 us
    dot_general x1, matrix products, local(): jnp.dot(tokens, weights_all, preferred_element_type=jnp.float32)  14.3 us
  transfers between devices with their start and end apart: 7, of which 5 were waited for; matrix products, arithmetic and copies ran while one was open for 21% of the time, Pallas kernels for 0%

profile of v1, /device:TPU:8, one launch (start us, length us, event | category | flops | bytes accessed | tf_op | source)
XLA Modules:
  0.0 333.7 jit_solution(14265051133832841151)
XLA Ops:
  8.0 1.3 copy.882
  9.3 1.2 copy.881
  10.8 0.9 copy.883
  11.7 11.3 %all-to-all-start = ((bf16[2,32,32,128]{3,2,0,1:T(8,128)(2,1)}), bf16[2,32,32,128]{3,2,0,1:T(8,128)(2,1)S(1)}, u32[]{:S(2)}, u32[]{:S(2)}) async-start(bf16[2,32,32,128]{3,2,0,1:T(8,128)(2,1)} %copy.883), calls=%async_computation.1 | async-start | bytes 1048576 | tf_op jit(solution)/shard_map/all_to_all | solution.py:45
  23.1 0.8 reshape.107
  24.0 16.8 %all-to-all-done = bf16[2,32,32,128]{3,2,0,1:T(8,128)(2,1)S(1)} async-done(((bf16[2,32,32,128]{3,2,0,1:T(8,128)(2,1)}), bf16[2,32,32,128]{3,2,0,1:T(8,128)(2,1)S(1)}, u32[]{:S(2)}, u32[]{:S(2)}) %all-to-all-start) | async-done | bytes 524320 | tf_op jit(solution)/shard_map/all_to_all | solution.py:45
  41.1 1.9 gather_fusion
  43.0 1.4 copy.934
  44.4 26.3 %all_to_all.50 = bf16[32,3,32,128]{3,2,1,0:T(8,128)(2,1)S(1)} all-to-all(bf16[32,3,32,128]{3,2,1,0:T(8,128)(2,1)S(1)} %bitcast.155), channel_id=1, replica_groups=mesh['dp'=32,'mp'=8] {'dp'}, dimensions={0} | all-to-all | bytes 1572864 | tf_op jit(solution)/shard_map/all_to_all | solution.py:49
  70.7 1.1 fusion.4
  71.8 1.4 fusion.5
  73.3 0.5 all-gather.3.cloned.1.call-update
  73.9 0.5 all-gather.5.cloned.1.call-update
  74.8 56.7 %all-reduce.3.cloned.1.call-done = (bf16[3,128,64]{1,2,0:T(8,128)(2,1)}, bf16[3,128,64]{1,2,0:T(8,128)(2,1)}) async-done(((bf16[3,128,64]{1,2,0:T(8,128)(2,1)}, bf16[3,128,64]{1,2,0:T(8,128)(2,1)}), (bf16[3,128,64]{1,2,0:T(8,128)(2,1)}, bf16[3,128,64]{1,2,0:T(8,128)(2,1)})) %all-reduce.3.cloned.1.call-update) | async-done | bytes 98320 | tf_op jit(solution)/shard_map/psum | solution.py:57
  131.5 1.1 fusion.3
  132.6 1.1 fusion.2
  134.2 0.9 copy.890
  135.1 9.5 %all-to-all-start.2 = ((bf16[3,32,32,128]{3,2,0,1:T(8,128)(2,1)}), bf16[3,32,32,128]{3,2,0,1:T(8,128)(2,1)S(1)}, u32[]{:S(2)}, u32[]{:S(2)}) async-start(bf16[3,32,32,128]{3,2,0,1:T(8,128)(2,1)} %copy.890), calls=%async_computation.3 | async-start | bytes 1572864 | tf_op jit(solution)/shard_map/all_to_all | solution.py:88
  144.7 30.5 %all-to-all-done.2 = bf16[3,32,32,128]{3,2,0,1:T(8,128)(2,1)S(1)} async-done(((bf16[3,32,32,128]{3,2,0,1:T(8,128)(2,1)}), bf16[3,32,32,128]{3,2,0,1:T(8,128)(2,1)S(1)}, u32[]{:S(2)}, u32[]{:S(2)}) %all-to-all-start.2) | async-done | bytes 786464 | tf_op jit(solution)/shard_map/all_to_all | solution.py:88
  175.3 63.4 %all-gather.3.cloned.1.call-done = bf16[1024,8192]{1,0:T(8,128)(2,1)} async-done(((bf16[1024,256]{1,0:T(8,128)(2,1)}), bf16[1024,8192]{1,0:T(8,128)(2,1)}) %all-gather.3.cloned.1.call-update) | async-done | bytes 16777232 | tf_op jit(solution)/shard_map/all_gather | solution.py:59
  238.7 14.3 %convolution_convert_fusion = bf16[384,8192]{1,0:T(8,128)(2,1)} fusion(bf16[384,1024]{1,0:T(8,128)(2,1)S(1)} %copy-done, bf16[1024,8192]{1,0:T(8,128)(2,1)} %all-gather.3.cloned.1.call-done), kind=kOutput, calls=%fused_computation.1 | convolution fusion | flops 6445596672 | bytes 23855104 | tf_op jit(solution)/shard_map/dot_general | solution.py:60
  253.9 0.6 constant_dynamic-update-slice_fusion.31
  254.5 0.6 constant_dynamic-update-slice_fusion.30
  255.1 0.6 constant_dynamic-update-slice_fusion.29
  255.7 0.6 constant_dynamic-update-slice_fusion.28
  256.4 0.6 constant_dynamic-update-slice_fusion.27
  257.0 0.6 constant_dynamic-update-slice_fusion.26
  257.6 0.6 constant_dynamic-update-slice_fusion.25
  258.2 0.6 constant_dynamic-update-slice_fusion.24
  258.8 0.6 constant_dynamic-update-slice_fusion.23
  259.4 0.6 constant_dynamic-update-slice_fusion.22
  260.0 0.6 constant_dynamic-update-slice_fusion.21
  260.6 0.6 constant_dynamic-update-slice_fusion.20
  261.2 0.6 constant_dynamic-update-slice_fusion.19
  261.8 0.7 fusion.25
  262.6 0.6 constant_dynamic-update-slice_fusion.18
  263.2 0.6 constant_dynamic-update-slice_fusion.17
  263.8 0.6 constant_dynamic-update-slice_fusion.16
  264.4 0.6 constant_dynamic-update-slice_fusion.15
  265.0 0.6 constant_dynamic-update-slice_fusion.14
  265.6 0.6 constant_dynamic-update-slice_fusion.13
  266.2 0.6 constant_dynamic-update-slice_fusion.12
  266.8 0.6 constant_dynamic-update-slice_fusion.11
  267.4 0.6 constant_dynamic-update-slice_fusion.10
  268.0 0.6 constant_dynamic-update-slice_fusion.9
  268.6 0.6 constant_dynamic-update-slice_fusion.8
  269.3 0.6 constant_dynamic-update-slice_fusion.7
  269.9 0.6 constant_dynamic-update-slice_fusion.6
  270.5 0.6 constant_dynamic-update-slice_fusion.5
  271.1 0.6 constant_dynamic-update-slice_fusion.4
  271.7 0.6 constant_dynamic-update-slice_fusion.3
  272.3 0.6 constant_dynamic-update-slice_fusion.2
  272.9 0.6 constant_dynamic-update-slice_fusion.1
  273.5 0.6 constant_dynamic-update-slice_fusion
  274.1 7.3 %all-to-all-start.3 = ((bf16[32,1,2,32,128]{4,3,2,1,0:T(8,128)(2,1)}), bf16[32,1,2,32,128]{4,3,2,1,0:T(8,128)(2,1)}, u32[]{:S(2)}, u32[]{:S(2)}) async-start(bf16[32,1,2,32,128]{4,3,2,1,0:T(8,128)(2,1)} %constant_dynamic-update-slice_fusion), calls=%async_computation.4 | async-start | bytes 1048576 | tf_op jit(solution)/shard_map/all_to_all | solution.py:12
  281.4 0.7 fusion.7
  282.2 1.7 fusion.11
  283.9 13.0 %all-to-all-done.3 = bf16[32,1,2,32,128]{4,3,2,1,0:T(8,128)(2,1)} async-done(((bf16[32,1,2,32,128]{4,3,2,1,0:T(8,128)(2,1)}), bf16[32,1,2,32,128]{4,3,2,1,0:T(8,128)(2,1)}, u32[]{:S(2)}, u32[]{:S(2)}) %all-to-all-start.3) | async-done | bytes 524320 | tf_op jit(solution)/shard_map/all_to_all | solution.py:12
  296.9 1.2 convert_bitcast_fusion
  298.2 1.6 fusion.24
  299.8 2.4 copy.895
  302.1 2.4 copy.896
  304.5 19.4 %fusion = bf16[384,1024]{1,0:T(8,128)(2,1)} fusion(f32[3,128,1024]{2,1,0:T(8,128)} %fusion.11, bf16[384,8192]{1,0:T(8,128)(2,1)} %all-gather.5.cloned.1.call-done, bf16[1024,8192]{1,0:T(8,128)(2,1)} %all-gather.3.cloned.1.call-done), kind=kOutput, calls=%fused_computation.3 | convolution fusion | flops 6443237376 | bytes 25427968 | tf_op jit(solution)/shard_map/dot_general | solution.py:75
  323.9 2.4 fusion.1
  (41 shorter events, 2.8 us)
Async XLA Ops:
  8.0 62.7 %copy-start = (bf16[384,1024]{1,0:T(8,128)(2,1)S(1)}, bf16[384,1024]{1,0:T(8,128)(2,1)}, u32[]{:S(2)}) copy-start(bf16[384,1024]{1,0:T(8,128)(2,1)} %param.7) | copy-start | bytes 2359300
  11.7 29.0 %all-to-all-start = ((bf16[2,32,32,128]{3,2,0,1:T(8,128)(2,1)}), bf16[2,32,32,128]{3,2,0,1:T(8,128)(2,1)S(1)}, u32[]{:S(2)}, u32[]{:S(2)}) async-start(bf16[2,32,32,128]{3,2,0,1:T(8,128)(2,1)} %copy.883), calls=%async_computation.1 | async-start | bytes 1048576 | tf_op jit(solution)/shard_map/all_to_all | solution.py:45
  23.0 108.4 %all-reduce.3.cloned.1.call-start = ((), (), s32[]{:S(2)}) async-start(), calls=%async_computation.8 | async-start | bytes 196608 | tf_op jit(solution)/shard_map/psum | solution.py:57
  41.1 30.8 %copy-start.1 = (bf16[384,1024]{1,0:T(8,128)(2,1)S(1)}, bf16[384,1024]{1,0:T(8,128)(2,1)}, u32[]{:S(2)}) copy-start(bf16[384,1024]{1,0:T(8,128)(2,1)} %param.11) | copy-start | bytes 2359300
  43.0 31.5 %copy-start.5 = (s32[96]{0:T(128)S(1)}, s32[96]{0:T(128)}, u32[]{:S(2)}) copy-start(s32[96]{0:T(128)} %param.12) | copy-start | bytes 1156
  43.0 31.6 %copy-start.6 = (s32[64]{0:T(128)S(1)}, s32[64]{0:T(128)}, u32[]{:S(2)}) copy-start(s32[64]{0:T(128)} %param.13) | copy-start | bytes 772
  43.0 88.5 %copy-start.2 = (bf16[384,1024]{1,0:T(8,128)(2,1)S(1)}, bf16[384,1024]{1,0:T(8,128)(2,1)}, u32[]{:S(2)}) copy-start(bf16[384,1024]{1,0:T(8,128)(2,1)} %param.11) | copy-start | bytes 2359300
  73.3 165.4 %all-gather.3.cloned.1.call-start = ((), (), s32[]{:S(2)}) async-start(), calls=%async_computation.5 | async-start | bytes 17301504 | tf_op jit(solution)/shard_map/all_gather | solution.py:59
  73.9 230.6 %all-gather.5.cloned.1.call-start = ((), (), s32[]{:S(2)}) async-start(), calls=%async_computation.7 | async-start | bytes 7077888 | tf_op jit(solution)/shard_map/all_gather | solution.py:74
  135.1 40.1 %all-to-all-start.2 = ((bf16[3,32,32,128]{3,2,0,1:T(8,128)(2,1)}), bf16[3,32,32,128]{3,2,0,1:T(8,128)(2,1)S(1)}, u32[]{:S(2)}, u32[]{:S(2)}) async-start(bf16[3,32,32,128]{3,2,0,1:T(8,128)(2,1)} %copy.890), calls=%async_computation.3 | async-start | bytes 1572864 | tf_op jit(solution)/shard_map/all_to_all | solution.py:88
  144.6 179.3 %reduce-scatter.2.cloned.1.call-start = ((), (), s32[]{:S(2)}) async-start(), calls=%async_computation.6 | async-start | bytes 7077888 | tf_op jit(solution)/shard_map/reduce_scatter | solution.py:61
  253.0 28.4 %copy-start.4 = (bf16[3,128,64]{1,2,0:T(8,128)(2,1)S(1)}, bf16[3,128,64]{1,2,0:T(8,128)(2,1)}, u32[]{:S(2)}) copy-start(bf16[3,128,64]{1,2,0:T(8,128)(2,1)} %get-tuple-element.132) | copy-start | bytes 147460
  253.0 29.1 %copy-start.3 = (bf16[3,128,64]{1,2,0:T(8,128)(2,1)S(1)}, bf16[3,128,64]{1,2,0:T(8,128)(2,1)}, u32[]{:S(2)}) copy-start(bf16[3,128,64]{1,2,0:T(8,128)(2,1)} %get-tuple-element.133) | copy-start | bytes 147460
  274.1 22.8 %all-to-all-start.3 = ((bf16[32,1,2,32,128]{4,3,2,1,0:T(8,128)(2,1)}), bf16[32,1,2,32,128]{4,3,2,1,0:T(8,128)(2,1)}, u32[]{:S(2)}, u32[]{:S(2)}) async-start(bf16[32,1,2,32,128]{4,3,2,1,0:T(8,128)(2,1)} %constant_dynamic-update-slice_fusion), calls=%async_computation.4 | async-start | bytes 1048576 | tf_op jit(solution)/shard_map/all_to_all | solution.py:12
Sparse Core Ops, SparseCore 0:
  73.4 58.0 all-reduce.2
  253.2 57.4 reduce-scatter.1
Sparse Core Ops, SparseCore 1:
  76.5 162.1 all-gather.2
  240.6 50.6 all-gather.4
